TPU v7x, 32 devices: a whole 2x2x4 slice. The times are simulated.
32 devices in a mesh: dp: 4 (over y, x), tm: 8 (over z, core).
Axes of the slice: x: 2, y: 2, z: 4, core: 2. Of those that a mesh axis runs over, the one named last changes fastest.
Arguments:
- clips: bfloat16 [4, 128, 512, 512], P('dp', 'tm'), may hold values from -6 to 6
- w_time: bfloat16 [3, 512, 512], P(None, 'dp'), may hold values from -0.15625 to 0.15625
- gain: float32 [512], replicated, may hold values from 0.1 to 1.9
- rate: float32 [512], replicated, may hold values from 0.000390625 to 0.0333333333
- keep: float32 [128], P('tm'), may hold values from 0.5 to 1
- latent_ids: int32 [128], P('tm'), may hold values from 0 to 15, as said below
- w_lat: bfloat16 [512, 16], replicated, may hold values from -0.25 to 0.25
Outputs:
- features: bfloat16 [4, 128, 512, 512], P('dp', 'tm')
- latents: float32 [4, 16, 16, 512], P('dp', 'tm')
Inputs may be any that keep to these rules, and one draw needn't show every extreme that they name: latent_ids never falls as the frame grows; latent frame j begins at a frame from j * 8 - 7 to j * 8 (latent 0 at frame 0) and ends where the next begins; every latent frame gets 1 to 15 frames and the last exactly 15.
All inputs are finite; a program needn't handle non-finite values.
Results may differ from a plain program's by a relative error of at most 0.0025.
Values may be sent and summed in bfloat16 or wider, within the bound.
A program may use at most 192 MiB of HBM per device.

v0:
```python
import jax
import jax.numpy as jnp
from jax import lax
from jax.sharding import PartitionSpec as P

KT = 3
STRIDE = 8


def shifted(value, axis, steps):
    count = lax.axis_size(axis)
    leading, last = (max(0, -steps), min(count, count - steps))
    return lax.ppermute(value, axis, [(source, source + steps) for source in range(leading, last)])


def entering(value, axis, join, neutral):
    count, mine = (lax.axis_size(axis), lax.axis_index(axis))
    pieces = jax.tree.map(lambda part: lax.all_gather(part, axis), value)
    so_far = jax.tree.map(
        lambda part, zero: jnp.full_like(part, 0) + jnp.asarray(zero, part.dtype), value, neutral
    )

    def entering_step(position, so_far):
        longer = join(so_far, jax.tree.map(lambda part: part[position], pieces))
        return jax.tree.map(lambda new, old: jnp.where(position < mine, new, old), longer, so_far)

    return lax.fori_loop(0, count - 1, entering_step, so_far)


def combine_pairs(earlier, later):
    return (earlier[0] * later[0], later[0] * earlier[1] + later[1])


def per_device(clips, w_time, gain, rate, keep, latent_ids, w_lat):
    nclip, nframe, npos, nchan = clips.shape
    tail = clips[:, nframe - (KT - 1) :]
    prior = shifted(tail, "tm", 1)
    padded = jnp.concatenate([prior, clips], 1)
    nrows = nclip * nframe * npos
    total = jnp.zeros((nrows, nchan), jnp.float32)
    piece = lax.all_gather(w_time, "dp", axis=1, tiled=True)
    width = piece.shape[1]
    for k in range(KT):
        part = padded[:, KT - 1 - k : KT - 1 - k + nframe]
        columns = part.reshape(nrows, width)
        total = total + jnp.dot(columns, piece[k], preferred_element_type=jnp.float32)
    conv = total
    conv = conv.reshape(nclip, nframe, npos, nchan)
    features = (clips.astype(jnp.float32) + jax.nn.silu(conv)).astype(jnp.bfloat16)
    values = features.astype(jnp.float32)
    normed = values * lax.rsqrt(jnp.mean(values * values, -1, keepdims=True) + 1e-06) * gain
    decay = jnp.exp(-rate)
    inject = jnp.sqrt(-jnp.expm1(-2.0 * rate))
    retain = decay[None, :] * keep[:, None]

    def body_step(carry, inputs):
        state, product = carry
        kept, entry = inputs
        state = kept * state + inject * entry
        product = product * kept
        return ((state, product), (state, product))

    zero_state = jnp.zeros((nclip, npos, nchan), jnp.float32)
    (last_state, last_product), (local_state, local_product) = lax.scan(
        body_step,
        (zero_state, jnp.ones((nchan,), jnp.float32)),
        (retain, jnp.moveaxis(normed, 1, 0)),
    )
    _, arriving_operand = entering(
        (last_product, last_state),
        "tm",
        combine_pairs,
        (jnp.ones((nchan,), jnp.float32), zero_state),
    )
    state = local_state + local_product[:, None, None, :] * arriving_operand[None]
    state_b = jnp.moveaxis(state, 0, 1).astype(jnp.bfloat16)
    proj = jnp.einsum("bfpc,cl->bflp", state_b, w_lat, preferred_element_type=jnp.float32)
    lat_dev = nframe // STRIDE
    window = lax.axis_index("tm") * lat_dev + jnp.arange(lat_dev + 1, dtype=jnp.int32)
    onehot = (latent_ids[:, None] == window[None, :]).astype(jnp.float32)
    running_totals = jnp.einsum("fj,bflp->bjlp", onehot, proj, precision=lax.Precision.HIGHEST)
    shard_counts = jnp.sum(onehot, 0)
    moved, moved_count = (
        shifted(running_totals[:, lat_dev:].astype(jnp.bfloat16), "tm", 1).astype(jnp.float32),
        shifted(shard_counts[lat_dev:].astype(jnp.bfloat16), "tm", 1).astype(jnp.float32),
    )
    sums = jnp.concatenate([running_totals[:, :1] + moved, running_totals[:, 1:lat_dev]], 1)
    counts = jnp.concatenate([shard_counts[:1] + moved_count, shard_counts[1:lat_dev]], 0)
    latents = sums / counts[None, :, None, None]
    return (features, latents)


def solution(mesh):
    return jax.shard_map(
        per_device,
        mesh=mesh,
        in_specs=(P("dp", "tm", None, None), P(None, "dp", None), P(), P(), P("tm"), P("tm"), P()),
        out_specs=(P("dp", "tm", None, None), P("dp", "tm", None, None)),
        check_vma=False,
    )
```

profile of v0, /device:TPU:17, one launch (start us, length us, event | category | flops | bytes accessed | tf_op | source)
XLA Modules:
  0.0 272.5 jit_solution(7666991608825144765)
XLA Ops:
  8.5 3.8 %collective-permute-start = (bf16[1,2,512,512]{3,2,1,0:T(8,128)(2,1)S(1)}, bf16[1,2,512,512]{3,2,1,0:T(8,128)(2,1)S(1)}, u32[]{:S(2)}, u32[]{:S(2)}) collective-permute-start(bf16[1,2,512,512]{3,2,1,0:T(8,128)(2,1)S(1)} %slice.39), channel_id=1, source_target_pairs={{0,1},{1,2},{2,3},{3,4},{4,5},{5,6},{6,7},{8,9},{9,10},{10,11},{11... | collective-permute-start | bytes 3145736 | tf_op jit(solution)/shard_map/ppermute | solution.py:13
  13.8 10.2 %collective-permute-done = bf16[1,2,512,512]{3,2,1,0:T(8,128)(2,1)S(1)} collective-permute-done((bf16[1,2,512,512]{3,2,1,0:T(8,128)(2,1)S(1)}, bf16[1,2,512,512]{3,2,1,0:T(8,128)(2,1)S(1)}, u32[]{:S(2)}, u32[]{:S(2)}) %collective-permute-start) | collective-permute-done | bytes 1048608 | tf_op jit(solution)/shard_map/ppermute | solution.py:13
  25.1 7.5 %constant_dynamic-update-slice_fusion = bf16[1,18,512,512]{3,2,1,0:T(8,128)(2,1)} fusion(bf16[1,18,512,512]{3,2,1,0:T(8,128)(2,1)} %constant_dynamic-update-slice_fusion.1, bf16[1,16,512,512]{3,2,1,0:T(8,128)(2,1)} %param.11), kind=kLoop, calls=%fused_computation.36 | loop fusion | bytes 16777216 | tf_op jit(solution)/shard_map/concatenate | solution.py:38
  32.6 11.5 %fusion.21 = (bf16[1,16,512,512]{3,2,1,0:T(8,128)(2,1)}, bf16[1,16,512,512]{3,2,1,0:T(8,128)(2,1)}) fusion(bf16[1,18,512,512]{3,2,1,0:T(8,128)(2,1)} %constant_dynamic-update-slice_fusion), kind=kLoop, calls=%fused_computation.47 | loop fusion | bytes 33554432 | tf_op jit(solution)/shard_map/slice | solution.py:44
  44.1 13.9 %fusion.13 = f32[8192,512]{1,0:T(8,128)} fusion(bf16[8192,512]{1,0:T(8,128)(2,1)} %bitcast.80, bf16[3,512,512]{2,1,0:T(8,128)(2,1)} %all-gather.6.cloned.1.call-done), kind=kOutput, calls=%fused_computation.25 | convolution fusion | flops 4294967296 | bytes 25690112 | tf_op jit(solution)/shard_map/dot_general | solution.py:46
  58.0 8.2 %fusion.14 = f32[8192,512]{1,0:T(8,128)} fusion(bf16[8192,512]{1,0:T(8,128)(2,1)S(1)} %bitcast.78, bf16[3,512,512]{2,1,0:T(8,128)(2,1)S(1)} %copy-done.3), kind=kOutput, calls=%fused_computation.27 | convolution fusion | flops 4294967296 | bytes 25690112 | tf_op jit(solution)/shard_map/dot_general | solution.py:46
  66.1 21.6 %add_add_fusion = f32[8192,512]{1,0:T(8,128)} fusion(f32[8192,512]{1,0:T(8,128)} %fusion.14, f32[8192,512]{1,0:T(8,128)} %fusion.13, bf16[8192,512]{1,0:T(8,128)(2,1)} %bitcast.79, bf16[3,512,512]{2,1,0:T(8,128)(2,1)S(1)} %copy-done.3), kind=kOutput, calls=%fused_computation.16 | convolution fusion | flops 4303355904 | bytes 59244544 | tf_op jit(solution)/shard_map/dot_general | solution.py:46
  87.8 10.8 %fusion.2 = (f32[16,512]{1,0:T(8,128)S(1)}, bf16[1,16,512,512]{3,2,1,0:T(8,128)(2,1)S(1)}) fusion(f32[1,16,512,512]{3,2,1,0:T(8,128)} %bitcast.75, bf16[1,16,512,512]{3,2,1,0:T(8,128)(2,1)} %param.11), kind=kLoop, calls=%fused_computation.11 | loop fusion | flops 41934848 | bytes 33587200 | tf_op jit(solution)/shard_map/reduce_sum | solution.py:51
  98.6 3.4 %copy-done.2 = bf16[1,16,512,512]{3,2,1,0:T(8,128)(2,1)} copy-done((bf16[1,16,512,512]{3,2,1,0:T(8,128)(2,1)}, bf16[1,16,512,512]{3,2,1,0:T(8,128)(2,1)S(1)}, u32[]{:S(2)}) %copy-start.2) | copy-done | bytes 8388632
  102.0 6.2 %fusion.4 = f32[16,1,512,512]{3,2,1,0:T(8,128)} fusion(bf16[1,16,512,512]{3,2,1,0:T(8,128)(2,1)S(1)} %get-tuple-element.245, f32[512]{0:T(512)S(1)} %copy-done.4, f32[16,512]{1,0:T(8,128)S(1)} %add_rsqrt_fusion), kind=kLoop, calls=%fused_computation.13 | loop fusion | flops 12582912 | bytes 25200640
  108.2 45.6 %while.31 = (s32[]{:T(128)}, f32[1,512,512]{2,1,0:T(8,128)S(1)}, f32[512]{0:T(512)S(1)}, f32[16,1,512,512]{3,2,1,0:T(8,128)}, f32[16,512]{1,0:T(8,128)S(1)}, /*i...) while((s32[]{:T(128)}, f32[1,512,512]{2,1,0:T(8,128)S(1)}, ...), condition=%wide.region_2.3_spmd.clone, body=%wide.region_1.2_spmd.clone.sunk | while | flops 1049603 | bytes 4213368 | solution.py:64
  108.2 2.8 %bitcast_dynamic-update-slice_fusion.2 = (f32[16,1,512,512]{3,2,1,0:T(8,128)}, f32[1,512,512]{2,1,0:T(8,128)S(1)}) fusion(f32[16,1,512,512]{3,2,1,0:T(8,128)} %get-tuple-element.351, s32[]{:T(128)} %get-tuple-element.348, f32[16,1,512,512]{3,2,1,0:T(8,128)} %get-tuple-element.365, f32[512]{0:T(512)S(1)} %get-tuple-element.364, ...), kind=kLoop, calls=%fused_computation.clone.1 | loop fusion | flops 1048576 | bytes 4198913 | tf_op jit(solution)/shard_map/while/body/jit(dynamic_update_index_in_dim)/dynamic_update_slice | solution.py:64
  128.1 2.8 %bitcast_dynamic-update-slice_fusion.2 = (f32[16,1,512,512]{3,2,1,0:T(8,128)}, f32[1,512,512]{2,1,0:T(8,128)S(1)}) fusion(f32[16,1,512,512]{3,2,1,0:T(8,128)} %get-tuple-element.351, s32[]{:T(128)} %get-tuple-element.348, f32[16,1,512,512]{3,2,1,0:T(8,128)} %get-tuple-element.365, f32[512]{0:T(512)S(1)} %get-tuple-element.364, ...), kind=kLoop, calls=%fused_computation.clone.1 | loop fusion | flops 1048576 | bytes 4198913 | tf_op jit(solution)/shard_map/while/body/jit(dynamic_update_index_in_dim)/dynamic_update_slice | solution.py:64
  131.0 2.8 %bitcast_dynamic-update-slice_fusion.2 = (f32[16,1,512,512]{3,2,1,0:T(8,128)}, f32[1,512,512]{2,1,0:T(8,128)S(1)}) fusion(f32[16,1,512,512]{3,2,1,0:T(8,128)} %get-tuple-element.351, s32[]{:T(128)} %get-tuple-element.348, f32[16,1,512,512]{3,2,1,0:T(8,128)} %get-tuple-element.365, f32[512]{0:T(512)S(1)} %get-tuple-element.364, ...), kind=kLoop, calls=%fused_computation.clone.1 | loop fusion | flops 1048576 | bytes 4198913 | tf_op jit(solution)/shard_map/while/body/jit(dynamic_update_index_in_dim)/dynamic_update_slice | solution.py:64
  133.9 2.8 %bitcast_dynamic-update-slice_fusion.2 = (f32[16,1,512,512]{3,2,1,0:T(8,128)}, f32[1,512,512]{2,1,0:T(8,128)S(1)}) fusion(f32[16,1,512,512]{3,2,1,0:T(8,128)} %get-tuple-element.351, s32[]{:T(128)} %get-tuple-element.348, f32[16,1,512,512]{3,2,1,0:T(8,128)} %get-tuple-element.365, f32[512]{0:T(512)S(1)} %get-tuple-element.364, ...), kind=kLoop, calls=%fused_computation.clone.1 | loop fusion | flops 1048576 | bytes 4198913 | tf_op jit(solution)/shard_map/while/body/jit(dynamic_update_index_in_dim)/dynamic_update_slice | solution.py:64
  139.6 2.8 %bitcast_dynamic-update-slice_fusion.2 = (f32[16,1,512,512]{3,2,1,0:T(8,128)}, f32[1,512,512]{2,1,0:T(8,128)S(1)}) fusion(f32[16,1,512,512]{3,2,1,0:T(8,128)} %get-tuple-element.351, s32[]{:T(128)} %get-tuple-element.348, f32[16,1,512,512]{3,2,1,0:T(8,128)} %get-tuple-element.365, f32[512]{0:T(512)S(1)} %get-tuple-element.364, ...), kind=kLoop, calls=%fused_computation.clone.1 | loop fusion | flops 1048576 | bytes 4198913 | tf_op jit(solution)/shard_map/while/body/jit(dynamic_update_index_in_dim)/dynamic_update_slice | solution.py:64
  142.5 2.8 %bitcast_dynamic-update-slice_fusion.2 = (f32[16,1,512,512]{3,2,1,0:T(8,128)}, f32[1,512,512]{2,1,0:T(8,128)S(1)}) fusion(f32[16,1,512,512]{3,2,1,0:T(8,128)} %get-tuple-element.351, s32[]{:T(128)} %get-tuple-element.348, f32[16,1,512,512]{3,2,1,0:T(8,128)} %get-tuple-element.365, f32[512]{0:T(512)S(1)} %get-tuple-element.364, ...), kind=kLoop, calls=%fused_computation.clone.1 | loop fusion | flops 1048576 | bytes 4198913 | tf_op jit(solution)/shard_map/while/body/jit(dynamic_update_index_in_dim)/dynamic_update_slice | solution.py:64
  145.4 2.8 %bitcast_dynamic-update-slice_fusion.2 = (f32[16,1,512,512]{3,2,1,0:T(8,128)}, f32[1,512,512]{2,1,0:T(8,128)S(1)}) fusion(f32[16,1,512,512]{3,2,1,0:T(8,128)} %get-tuple-element.351, s32[]{:T(128)} %get-tuple-element.348, f32[16,1,512,512]{3,2,1,0:T(8,128)} %get-tuple-element.365, f32[512]{0:T(512)S(1)} %get-tuple-element.364, ...), kind=kLoop, calls=%fused_computation.clone.1 | loop fusion | flops 1048576 | bytes 4198913 | tf_op jit(solution)/shard_map/while/body/jit(dynamic_update_index_in_dim)/dynamic_update_slice | solution.py:64
  148.2 2.8 %bitcast_dynamic-update-slice_fusion.2 = (f32[16,1,512,512]{3,2,1,0:T(8,128)}, f32[1,512,512]{2,1,0:T(8,128)S(1)}) fusion(f32[16,1,512,512]{3,2,1,0:T(8,128)} %get-tuple-element.351, s32[]{:T(128)} %get-tuple-element.348, f32[16,1,512,512]{3,2,1,0:T(8,128)} %get-tuple-element.365, f32[512]{0:T(512)S(1)} %get-tuple-element.364, ...), kind=kLoop, calls=%fused_computation.clone.1 | loop fusion | flops 1048576 | bytes 4198913 | tf_op jit(solution)/shard_map/while/body/jit(dynamic_update_index_in_dim)/dynamic_update_slice | solution.py:64
  155.7 4.3 %collective-permute-start.2 = (bf16[1]{0:T(256)(128)(2,1)}, bf16[1]{0:T(256)(128)(2,1)}, u32[]{:S(2)}, u32[]{:S(2)}) collective-permute-start(bf16[1]{0:T(256)(128)(2,1)} %slice.48), channel_id=1, source_target_pairs={{0,1},{1,2},{2,3},{3,4},{4,5},{5,6},{6,7},{8,9},{9,10},{10,11},{11... | collective-permute-start | bytes 14 | tf_op jit(solution)/shard_map/ppermute | solution.py:13
  162.2 14.4 %all-gather.2 = f32[8,1,512]{2,1,0:T(1,128)S(1)} all-gather(f32[1,1,512]{2,1,0:T(1,128)S(1)} %bitcast.86), channel_id=2, replica_groups=mesh['dp'=4,'tm'=8] {'tm'}, dimensions={0}, use_global_device_ids=true | all-gather | bytes 18432 | tf_op jit(solution)/shard_map/all_gather | solution.py:18
  176.6 61.3 %all-gather.8.cloned.1.call-done = f32[8,512,512]{2,1,0:T(8,128)} async-done(((f32[1,512,512]{2,1,0:T(8,128)}), f32[8,512,512]{2,1,0:T(8,128)}) %all-gather.8.cloned.1.call-update) | async-done | bytes 8388624 | tf_op jit(solution)/shard_map/all_gather | solution.py:18
  237.8 15.2 %while.32 = (s32[]{:T(128)}, f32[1,512,512]{2,1,0:T(8,128)S(1)}, s32[]{:T(128)}, f32[8,512]{1,0:T(8,128)S(1)}, f32[8,1,512,512]{3,2,1,0:T(8,128)}, /*index=5*/s32[]{:T(128)}, s32[]{:T(128)}) while((s32[]{:T(128)}, f32[1,512,512]{2,1,0:T(8,128)S(1)}, s32[]{:T(128)}, f32[8,512]{1,0:T(8,128)S(1)}, f32[8,1,512,512]{3,2,1,0:T(8,128)}, ...), condition=%wide.region_4.5_spmd.clone, body=%wide.region_3.4_spmd.clone.sunk | while | flops 1048580 | bytes 3151977 | solution.py:27
  253.0 8.1 %fusion.10 = f32[16,16,512]{2,1,0:T(8,128)S(1)} fusion(f32[16,1,512,512]{3,2,1,0:T(8,128)} %get-tuple-element.141, f32[512,512]{1,0:T(8,128)S(1)} %bitcast.81, f32[16,512]{1,0:T(8,128)S(1)} %get-tuple-element.142, bf16[512,16]{0,1:T(8,128)(2,1)S(1)} %copy-done), kind=kOutput, calls=%fused_computation.21 | convolution fusion | flops 146800640 | bytes 18399232 | tf_op jit(solution)/shard_map/bfpc,cl->bflp/dot_general | solution.py:77
  (116 shorter events, 48.9 us)
Async XLA Ops:
  7.2 245.9 %copy-start = (bf16[512,16]{0,1:T(8,128)(2,1)S(1)}, bf16[512,16]{0,1:T(8,128)(2,1)}, u32[]{:S(2)}) copy-start(bf16[512,16]{0,1:T(8,128)(2,1)} %param.17) | copy-start | bytes 49156
  7.2 36.9 %all-gather.6.cloned.1.call-start = ((), (), s32[]{:S(2)}) async-start(), calls=%async_computation | async-start | bytes 1966080 | tf_op jit(solution)/shard_map/all_gather | solution.py:41
  8.5 15.5 %collective-permute-start = (bf16[1,2,512,512]{3,2,1,0:T(8,128)(2,1)S(1)}, bf16[1,2,512,512]{3,2,1,0:T(8,128)(2,1)S(1)}, u32[]{:S(2)}, u32[]{:S(2)}) collective-permute-start(bf16[1,2,512,512]{3,2,1,0:T(8,128)(2,1)S(1)} %slice.39), channel_id=1, source_target_pairs={{0,1},{1,2},{2,3},{3,4},{4,5},{5,6},{6,7},{8,9},{9,10},{10,11},{11... | collective-permute-start | bytes 3145736 | tf_op jit(solution)/shard_map/ppermute | solution.py:13
  12.3 225.5 %all-gather.8.cloned.1.call-start = ((), (), s32[]{:S(2)}) async-start(), calls=%async_computation.1 | async-start | bytes 9437184 | tf_op jit(solution)/shard_map/all_gather | solution.py:18
  44.1 13.9 %slice-start = ((s8[8388608]{0:T(1024)(128)(4,1)}), s8[4194304]{0:T(1024)(128)(4,1)S(1)}, s32[]{:S(2)}) async-start(s8[8388608]{0:T(1024)(128)(4,1)} %bitcast.76), calls=%async_computation.2 | async-start | bytes 8388608
  44.1 13.9 %copy-start.3 = (bf16[3,512,512]{2,1,0:T(8,128)(2,1)S(1)}, bf16[3,512,512]{2,1,0:T(8,128)(2,1)}, u32[]{:S(2)}) copy-start(bf16[3,512,512]{2,1,0:T(8,128)(2,1)} %all-gather.6.cloned.1.call-done) | copy-start | bytes 4718596
  44.1 13.9 %slice-start.1 = ((s8[8388608]{0:T(1024)(128)(4,1)}), s8[4194304]{0:T(1024)(128)(4,1)S(1)}, s32[]{:S(2)}) async-start(s8[8388608]{0:T(1024)(128)(4,1)} %bitcast.76), calls=%async_computation.3 | async-start | bytes 8388608
  87.8 14.2 %copy-start.4 = (f32[512]{0:T(512)S(1)}, f32[512]{0:T(512)}, u32[]{:S(2)}) copy-start(f32[512]{0:T(512)} %param.13) | copy-start | bytes 6148
  98.6 3.4 %copy-start.2 = (bf16[1,16,512,512]{3,2,1,0:T(8,128)(2,1)}, bf16[1,16,512,512]{3,2,1,0:T(8,128)(2,1)S(1)}, u32[]{:S(2)}) copy-start(bf16[1,16,512,512]{3,2,1,0:T(8,128)(2,1)S(1)} %get-tuple-element.245) | copy-start | bytes 25165828
  108.2 46.8 %copy-start.5 = (s32[16]{0:T(128)S(1)}, s32[16]{0:T(128)}, u32[]{:S(2)}) copy-start(s32[16]{0:T(128)} %param.16) | copy-start | bytes 196
  153.9 1.1 copy-start.1
  155.7 5.1 %collective-permute-start.2 = (bf16[1]{0:T(256)(128)(2,1)}, bf16[1]{0:T(256)(128)(2,1)}, u32[]{:S(2)}, u32[]{:S(2)}) collective-permute-start(bf16[1]{0:T(256)(128)(2,1)} %slice.48), channel_id=1, source_target_pairs={{0,1},{1,2},{2,3},{3,4},{4,5},{5,6},{6,7},{8,9},{9,10},{10,11},{11... | collective-permute-start | bytes 14 | tf_op jit(solution)/shard_map/ppermute | solution.py:13
  261.8 3.1 %collective-permute-start.1 = (bf16[1,1,16,512]{3,1,2,0:T(2,128)(2,1)S(1)}, bf16[1,1,16,512]{3,1,2,0:T(2,128)(2,1)S(1)}, u32[]{:S(2)}, u32[]{:S(2)}) collective-permute-start(bf16[1,1,16,512]{3,1,2,0:T(2,128)(2,1)S(1)} %slice.66), channel_id=1, source_target_pairs={{0,1},{1,2},{2,3},{3,4},{4,5},{5,6},{6,7},{8,9},{9,10},{10,11},{11... | collective-permute-start | bytes 49160 | tf_op jit(solution)/shard_map/ppermute | solution.py:13
Sparse Core Ops, SparseCore 0:
  12.4 30.5 all-gather.5
  155.1 82.7 all-gather.7
where the time goes:
time: 276 us; the launch traced here: 273 us
  other arithmetic  78.8 us (29%)
  waiting for transfers between devices  72 us (26%)
  matrix products  52.3 us (19%)
  local copies, waits for them, and re-layouts  28.5 us (10%)
  between operations  15.6 us (6%)
  blocking collectives  14.4 us (5%)
  starting transfers between devices  10.2 us (4%)
    all_gather x1, waiting for transfers between devices, entering(): pieces = jax.tree.map(lambda part: lax.all_gather(part, axis), value)  61.3 us
    dynamic_update_slice x16, other arithmetic, per_device(): lax.scan(body_step, (zero_state, jnp.ones((nchan,), jnp.float32)), (retai...  44.2 us
    dot_general x3, matrix products, per_device(): jnp.dot(columns, piece[k], preferred_element_type=jnp.float32)  43.7 us
    select_n x7, other arithmetic, entering_step(): jnp.where(position < mine, new, old)  15 us
    all_gather x1, blocking collectives, entering(): pieces = jax.tree.map(lambda part: lax.all_gather(part, axis), value)  14.4 us
    slice x1, local copies, waits for them, and re-layouts, per_device(): part = padded[:, KT - 1 - k:KT - 1 - k + nframe]  11.5 us
    reduce_sum x1, other arithmetic, per_device(): jnp.mean(values * values, -1, keepdims=True) + 1e-06  10.8 us
    ppermute x3, waiting for transfers between devices, shifted(): lax.ppermute(value, axis, [(source, source + steps) for source in range(l...  10.7 us
  transfers between devices with their start and end apart: 5, of which 4 were waited for; matrix products, arithmetic and copies ran while one was open for 9% of the time, Pallas kernels for 0%

commit v1 on v0

v1 whole, which is shorter than its diff:
```python
import functools
import jax
import jax.numpy as jnp
from jax import lax
from jax.experimental import pallas as pl
from jax.experimental.pallas import tpu as pltpu
from jax.sharding import PartitionSpec as P

KT = 3
STRIDE = 8
NT = (((1,), (1,)), ((), ()))
HI = lax.Precision.HIGHEST


def build_maps(nframe, nlat, base, keep_row, ids_row, keep_own, ids_own, rate_col, gain_col, wl, out_ref):
    nall = keep_row.shape[1]
    ncol = wl.shape[1]
    width = ncol // nlat
    end = base + nframe - 1
    frame = lax.broadcasted_iota(jnp.int32, (8, nall), 1)
    later = frame > end
    logs = jnp.where(later, jnp.log(keep_row), 0.0)
    tri = (lax.broadcasted_iota(jnp.int32, (nall, nall), 0) <= lax.broadcasted_iota(jnp.int32, (nall, nall), 1)).astype(jnp.float32)
    cum = jnp.dot(logs, tri, precision=HI, preferred_element_type=jnp.float32)[:1]
    steps = (frame[:1] - end).astype(jnp.float32)
    power = jnp.where(later[:1], cum - rate_col * steps, -200.0)
    dec = jnp.exp(power)
    pooled = (lax.broadcasted_iota(jnp.int32, (ncol, nall), 0) // width == ids_row).astype(jnp.float32)
    entry = lax.dot_general(dec, pooled, NT, precision=HI, preferred_element_type=jnp.float32)
    counts = lax.dot_general(jnp.ones((8, nall), jnp.float32), pooled, NT, preferred_element_type=jnp.float32)[:1]
    inject = jnp.sqrt(1.0 - jnp.exp(-2.0 * rate_col))
    small = 2.0 * rate_col
    series = small * (1.0 - small * (0.5 - small * (1.0 / 6.0 - small * (1.0 / 24.0 - small * (1.0 / 120.0)))))
    inject = jnp.where(small < 0.125, jnp.sqrt(series), inject)
    weight = wl * (inject * gain_col) / counts
    decay = jnp.exp(-rate_col)
    column = lax.broadcasted_iota(jnp.int32, (1, ncol), 1) // width
    here = (column == ids_own(nframe - 1)).astype(jnp.float32)
    total = here + entry
    out_ref[nframe - 1] = (weight * total).astype(jnp.bfloat16)
    for g in range(nframe - 2, -1, -1):
        here = (column == ids_own(g)).astype(jnp.float32)
        total = here + (decay * keep_own(g + 1)) * total
        out_ref[g] = (weight * total).astype(jnp.bfloat16)


def maps_kernel(nlat, keep_own, ids_own, keep_row, ids_row, rate_col, gain_col, wl, out_ref):
    nframe = out_ref.shape[0]
    base = lax.axis_index("tm") * nframe
    build_maps(
        nframe, nlat, base, keep_row[...], ids_row[...],
        lambda g: keep_own[g], lambda g: ids_own[g],
        rate_col[...], gain_col[...], wl[...], out_ref,
    )


def main_kernel(rows, clips, prior, w, maps, features, acc, xbuf, sems):
    step = pl.program_id(0)
    nframe = clips.shape[0]
    npos = clips.shape[1]
    halo = KT - 1

    def load(slot):
        source = prior.at[slot] if slot < halo else clips.at[slot - halo]
        return pltpu.make_async_copy(source, xbuf.at[slot], sems.at[slot])

    @pl.when(step == 0)
    def _():
        for slot in range(nframe + halo):
            load(slot).start()
        for slot in range(halo):
            load(slot).wait()
        acc[...] = jnp.zeros_like(acc)

    pltpu.make_async_copy(clips.at[step], xbuf.at[step + halo], sems.at[step + halo]).wait()
    for at in range(0, npos, rows):
        span = slice(at, at + rows)
        own = xbuf[step + halo, span]
        lhs = jnp.concatenate([own] + [xbuf[step + halo - k, span] for k in range(1, KT)], axis=1)
        half = 0.5 * jnp.dot(lhs, w[...], preferred_element_type=jnp.float32)
        value = own.astype(jnp.float32) + (half * jnp.tanh(half) + half)
        rounded = value.astype(jnp.bfloat16)
        features[0, span] = rounded
        kept = rounded.astype(jnp.float32)
        scale = lax.rsqrt(jnp.mean(kept * kept, axis=-1, keepdims=True) + 1e-06)
        acc[span] += scale * jnp.dot(rounded, maps[0], preferred_element_type=jnp.float32)


def main_call(clips, prior, w, maps, rows=512):
    nframe, npos, nchan = clips.shape
    ncol = maps.shape[-1]
    halo = KT - 1
    return pl.pallas_call(
        functools.partial(main_kernel, rows),
        grid=(nframe,),
        out_shape=(
            jax.ShapeDtypeStruct((nframe, npos, nchan), jnp.bfloat16),
            jax.ShapeDtypeStruct((npos, ncol), jnp.float32),
        ),
        in_specs=[
            pl.BlockSpec(memory_space=pl.ANY),
            pl.BlockSpec(memory_space=pl.ANY),
            pl.BlockSpec(w.shape, lambda i: (0, 0)),
            pl.BlockSpec((1, nchan, ncol), lambda i: (i, 0, 0)),
        ],
        out_specs=(
            pl.BlockSpec((1, npos, nchan), lambda i: (i, 0, 0)),
            pl.BlockSpec((npos, ncol), lambda i: (0, 0)),
        ),
        scratch_shapes=[
            pltpu.VMEM((nframe + halo, npos, nchan), jnp.bfloat16),
            pltpu.SemaphoreType.DMA((nframe + halo,)),
        ],
        compiler_params=pltpu.CompilerParams(vmem_limit_bytes=48 * 1024 * 1024),
    )(clips, prior, w, maps)


def per_device(clips, w_time, gain, rate, keep, latent_ids, w_lat):
    nclip, nframe, npos, nchan = clips.shape
    ntm = lax.axis_size("tm")
    nlat = nframe * ntm // STRIDE
    latc = w_lat.shape[1]
    halo = KT - 1
    tail = clips[:, nframe - halo:]
    prior = lax.ppermute(tail, "tm", [(s, s + 1) for s in range(ntm - 1)])[0]
    w = lax.all_gather(w_time, "dp", axis=1, tiled=True).reshape(KT * nchan, nchan)
    keep_all = lax.all_gather(keep, "tm", tiled=True)
    ids_all = lax.all_gather(latent_ids, "tm", tiled=True)
    wl = jnp.tile(w_lat.astype(jnp.float32), (1, nlat))
    maps = pl.pallas_call(
        functools.partial(maps_kernel, nlat),
        out_shape=jax.ShapeDtypeStruct((nframe, nchan, nlat * latc), jnp.bfloat16),
        in_specs=[pl.BlockSpec(memory_space=pltpu.SMEM)] * 2 + [pl.BlockSpec(memory_space=pltpu.VMEM)] * 5,
        out_specs=pl.BlockSpec(memory_space=pltpu.VMEM),
        compiler_params=pltpu.CompilerParams(vmem_limit_bytes=60 * 1024 * 1024),
    )(keep, latent_ids, keep_all[None], ids_all[None], rate[:, None], gain[:, None], wl)
    features, acc = main_call(clips[0], prior, w, maps)
    share = acc.T.reshape(nlat, latc, npos)
    latents = lax.psum_scatter(share, "tm", scatter_dimension=0, tiled=True)
    return (features[None], latents[None])


def solution(mesh):
    return jax.shard_map(
        per_device,
        mesh=mesh,
        in_specs=(P("dp", "tm", None, None), P(None, "dp", None), P(), P(), P("tm"), P("tm"), P()),
        out_specs=(P("dp", "tm", None, None), P("dp", "tm", None, None)),
        check_vma=False,
    )
```

time: 276 us -> 116 us (0.42)
  the two profiles are of different devices: /device:TPU:17 before, /device:TPU:0 now
where the time goes in v1:
time: 116 us; the launch traced here: 115 us
  waiting for transfers between devices  33.2 us (29%)
  Pallas kernels  29.7 us (26%)
  blocking collectives  23.7 us (20%)
  between operations  14.7 us (13%)
  local copies, waits for them, and re-layouts  11.5 us (10%)
  starting transfers between devices  2.5 us (2%)
    reduce_scatter x1, waiting for transfers between devices, per_device(): latents = lax.psum_scatter(share, 'tm', scatter_dimension=0, tiled=True)  32.5 us
    pallas_call x1, Pallas kernels, main_call(): pl.pallas_call(functools.partial(main_kernel, rows), grid=(nframe,), out_...  24.4 us
    unnamed x2, blocking collectives  23.7 us
    pallas_call x1, Pallas kernels, per_device(): pl.pallas_call(functools.partial(maps_kernel, nlat), out_shape=jax.ShapeD...  5.31 us
    unnamed x7, local copies, waits for them, and re-layouts  4.35 us
    ppermute x1, starting transfers between devices, per_device(): prior = lax.ppermute(tail, 'tm', [(s, s + 1) for s in range(ntm - 1)])[0]  2.42 us
  transfers between devices with their start and end apart: 3, of which 1 were waited for; matrix products, arithmetic and copies ran while one was open for 8% of the time, Pallas kernels for 5%

profile of v1, /device:TPU:0, one launch (start us, length us, event | category | flops | bytes accessed | tf_op | source)
XLA Modules:
  0.0 115.4 jit_solution(17969123879027703529)
XLA Ops:
  7.2 0.0 all-gather.2.cloned.1.call-start
  7.2 0.7 all-gather.2.cloned.1.call-update
  7.9 0.0 reduce-scatter.2.cloned.1.call-start
  7.9 1.3 %slice.3 = bf16[1,2,512,512]{3,2,1,0:T(8,128)(2,1)S(1)} slice(bf16[1,16,512,512]{3,2,1,0:T(8,128)(2,1)} %param.7), slice={[0:1], [14:16], [0:512], [0:512]} | slice | bytes 2097152 | tf_op jit(solution)/shard_map/slice | solution.py:124
  9.2 2.4 %collective-permute-start = (bf16[1,2,512,512]{3,2,1,0:T(8,128)(2,1)S(1)}, bf16[1,2,512,512]{3,2,1,0:T(8,128)(2,1)S(1)}, u32[]{:S(2)}, u32[]{:S(2)}) collective-permute-start(bf16[1,2,512,512]{3,2,1,0:T(8,128)(2,1)S(1)} %slice.3), channel_id=1, source_target_pairs={{0,1},{1,2},{2,3},{3,4},{4,5},{5,6},{6,7},{8,9},{9,10},{10,11},{11... | collective-permute-start | bytes 3145736 | tf_op jit(solution)/shard_map/ppermute | solution.py:125
  11.7 1.6 %copy.12.gain_col = f32[512,1]{1,0:T(8,128)} copy(f32[512,1]{0,1:T(1,128)} %bitcast.19) | data formatting | bytes 4096 | tf_op jit(solution)/shard_map/broadcast_in_dim | solution.py:136
  13.2 1.6 %copy.11.rate_col = f32[512,1]{1,0:T(8,128)} copy(f32[512,1]{0,1:T(1,128)} %bitcast.20) | data formatting | bytes 4096 | tf_op jit(solution)/shard_map/broadcast_in_dim | solution.py:136
  14.8 0.8 tile.4
  15.6 1.0 copy.13.wl
  16.6 1.2 %dynamic-slice = u32[1]{0:T(128)} dynamic-slice(u32[32]{0:T(128)} %constant.3, u32[]{:T(128)S(6)} %add.2), dynamic_slice_sizes={1} | dynamic-slice | bytes 12
  18.5 0.9 dynamic-update-slice
  19.3 0.8 dynamic-update-slice.1
  20.2 17.6 %all-reduce = f32[128]{0:T(128)} all-reduce(f32[128]{0:T(128)S(1)} %dynamic-update-slice), channel_id=1, replica_groups=mesh['dp'=4,'tm'=8] {'tm'}, use_global_device_ids=true, to_apply=%add | all-reduce | flops 128 | bytes 1024
  37.8 6.1 %all-reduce.1 = s32[128]{0:T(128)} all-reduce(s32[128]{0:T(128)S(1)} %dynamic-update-slice.1), channel_id=1, replica_groups=mesh['dp'=4,'tm'=8] {'tm'}, use_global_device_ids=true, to_apply=%add.1 | all-reduce | flops 128 | bytes 1024
  43.9 5.3 %shard_map.86.maps = bf16[16,512,256]{2,1,0:T(8,128)(2,1)} custom-call(f32[16]{0:T(128)} %keep_own.1, s32[16]{0:T(128)} %ids_own.1, f32[1,128]{1,0:T(1,128)} %bitcast.21, s32[1,128]{1,0:T(1,128)} %bitcast.22, f32[512,1]{1,0:T(8,128)} %copy.11.rate_col, f32[512,1]{1,0:T(8,128)} %copy.12.gain_col, f32[512,256]{1,0:T(8,128)} %copy.13.wl), custom_call_target="tpu_custom_call" | custom-call | tf_op jit(solution)/shard_map/pallas_call | solution.py:130
  49.2 0.0 collective-permute-done
  49.2 0.0 all-gather.2.cloned.1.call-done
  49.2 0.0 copy-start
  49.2 1.4 %copy-done = bf16[3,512,512]{2,1,0:T(8,128)(2,1)S(1)} copy-done((bf16[3,512,512]{2,1,0:T(8,128)(2,1)S(1)}, bf16[3,512,512]{2,1,0:T(8,128)(2,1)}, u32[]{:S(2)}) %copy-start) | copy-done | bytes 1572888
  50.6 24.4 %shard_map.87 = (bf16[16,512,512]{2,1,0:T(8,128)(2,1)}, f32[512,256]{1,0:T(8,128)S(1)}) custom-call(bf16[16,512,512]{2,1,0:T(8,128)(2,1)} %bitcast.16, bf16[2,512,512]{2,1,0:T(8,128)(2,1)S(1)} %bitcast.14, bf16[1536,512]{1,0:T(8,128)(2,1)S(1)} %bitcast.13, bf16[16,512,256]{2,1,0:T(8,128)(2,1)} %shard_map.86.maps), custom_call_target="tpu_custom_call" | custom-call | tf_op jit(solution)/shard_map/pallas_call | solution.py:93
  75.0 1.0 copy.14
  76.0 0.0 reduce-scatter.2.cloned.1.call-update
  76.0 32.5 %reduce-scatter.2.cloned.1.call-done = f32[2,16,512]{2,1,0:T(8,128)} async-done(((f32[16,16,512]{2,1,0:T(8,128)}), f32[2,16,512]{2,1,0:T(8,128)}) %reduce-scatter.2.cloned.1.call-update) | async-done | bytes 65552 | tf_op jit(solution)/shard_map/reduce_scatter | solution.py:139
  (2 shorter events, 0.0 us)
Async XLA Ops:
  7.2 42.1 %all-gather.2.cloned.1.call-start = ((), (), s32[]{:S(2)}) async-start(), calls=%async_computation.1 | async-start | bytes 1966080 | tf_op jit(solution)/shard_map/all_gather | solution.py:126
  7.9 100.6 %reduce-scatter.2.cloned.1.call-start = ((), (), s32[]{:S(2)}) async-start(), calls=%async_computation.2 | async-start | bytes 589824 | tf_op jit(solution)/shard_map/reduce_scatter | solution.py:139
  9.2 40.0 %collective-permute-start = (bf16[1,2,512,512]{3,2,1,0:T(8,128)(2,1)S(1)}, bf16[1,2,512,512]{3,2,1,0:T(8,128)(2,1)S(1)}, u32[]{:S(2)}, u32[]{:S(2)}) collective-permute-start(bf16[1,2,512,512]{3,2,1,0:T(8,128)(2,1)S(1)} %slice.3), channel_id=1, source_target_pairs={{0,1},{1,2},{2,3},{3,4},{4,5},{5,6},{6,7},{8,9},{9,10},{10,11},{11... | collective-permute-start | bytes 3145736 | tf_op jit(solution)/shard_map/ppermute | solution.py:125
  49.2 1.4 %copy-start = (bf16[3,512,512]{2,1,0:T(8,128)(2,1)S(1)}, bf16[3,512,512]{2,1,0:T(8,128)(2,1)}, u32[]{:S(2)}) copy-start(bf16[3,512,512]{2,1,0:T(8,128)(2,1)} %all-gather.2.cloned.1.call-done) | copy-start | bytes 4718596
Sparse Core Ops, SparseCore 0:
  9.8 33.7 all-gather.1
  76.1 32.3 reduce-scatter.1

commit v2 on v1

--- a/solution.py
+++ b/solution.py
@@ -12,10 +12,17 @@
 HI = lax.Precision.HIGHEST
 
 
-def build_maps(nframe, nlat, base, keep_row, ids_row, keep_own, ids_own, rate_col, gain_col, wl, out_ref):
+MESH = pl.DeviceIdType.MESH
+
+
+def maps_of(nframe, nlat, base, keep_row, ids_row, keep_own, ids_own, rate_row, gain_row, w_lat, out_ref):
     nall = keep_row.shape[1]
-    ncol = wl.shape[1]
-    width = ncol // nlat
+    nchan, latc = w_lat.shape
+    ncol = nlat * latc
+    rate_col = jnp.broadcast_to(rate_row, (128, nchan)).T[:, :1]
+    gain_col = jnp.broadcast_to(gain_row, (128, nchan)).T[:, :1]
+    spread = lax.broadcasted_iota(jnp.int32, (latc, ncol), 1) % latc == lax.broadcasted_iota(jnp.int32, (latc, ncol), 0)
+    wl = jnp.dot(w_lat, spread.astype(jnp.bfloat16), preferred_element_type=jnp.float32)
     end = base + nframe - 1
     frame = lax.broadcasted_iota(jnp.int32, (8, nall), 1)
     later = frame > end
@@ -25,7 +32,7 @@
     steps = (frame[:1] - end).astype(jnp.float32)
     power = jnp.where(later[:1], cum - rate_col * steps, -200.0)
     dec = jnp.exp(power)
-    pooled = (lax.broadcasted_iota(jnp.int32, (ncol, nall), 0) // width == ids_row).astype(jnp.float32)
+    pooled = (lax.broadcasted_iota(jnp.int32, (ncol, nall), 0) // latc == ids_row).astype(jnp.float32)
     entry = lax.dot_general(dec, pooled, NT, precision=HI, preferred_element_type=jnp.float32)
     counts = lax.dot_general(jnp.ones((8, nall), jnp.float32), pooled, NT, preferred_element_type=jnp.float32)[:1]
     inject = jnp.sqrt(1.0 - jnp.exp(-2.0 * rate_col))
@@ -34,7 +41,7 @@
     inject = jnp.where(small < 0.125, jnp.sqrt(series), inject)
     weight = wl * (inject * gain_col) / counts
     decay = jnp.exp(-rate_col)
-    column = lax.broadcasted_iota(jnp.int32, (1, ncol), 1) // width
+    column = lax.broadcasted_iota(jnp.int32, (1, ncol), 1) // latc
     here = (column == ids_own(nframe - 1)).astype(jnp.float32)
     total = here + entry
     out_ref[nframe - 1] = (weight * total).astype(jnp.bfloat16)
@@ -44,14 +51,158 @@
         out_ref[g] = (weight * total).astype(jnp.bfloat16)
 
 
-def maps_kernel(nlat, keep_own, ids_own, keep_row, ids_row, rate_col, gain_col, wl, out_ref):
-    nframe = out_ref.shape[0]
-    base = lax.axis_index("tm") * nframe
-    build_maps(
-        nframe, nlat, base, keep_row[...], ids_row[...],
-        lambda g: keep_own[g], lambda g: ids_own[g],
-        rate_col[...], gain_col[...], wl[...], out_ref,
-    )
+def gather_kernel(ntm, nlat, clips, w_time, keep_s, ids_s, keep_v, ids_v, rate, gain, w_lat,
+                  w_full, prior, maps, small, zeros, local_sem, sw, rw, st, rt, sk, rk):
+    halo = KT - 1
+    nframe = clips.shape[0]
+    shard = w_time.shape[1]
+    d, t = lax.axis_index("dp"), lax.axis_index("tm")
+    c = lax.rem(t, 2)
+    sister = t + 1 - 2 * c
+    xd = d + 1 - 2 * lax.rem(d, 2)
+    yd = lax.rem(d + 2, 4)
+    part = shard // 4
+
+    barrier = pltpu.get_barrier_semaphore()
+    for k in range(1, ntm):
+        pl.semaphore_signal(barrier, inc=1, device_id=(d, lax.rem(t + k, ntm)), device_id_type=MESH)
+    for other in (xd, yd):
+        pl.semaphore_signal(barrier, inc=1, device_id=(other, t), device_id_type=MESH)
+    own_copy = pltpu.make_async_copy(w_time, w_full.at[:, pl.ds(d * shard, shard)], local_sem.at[0])
+    own_copy.start()
+    nall = small.shape[-1]
+    place = lax.broadcasted_iota(jnp.int32, (nframe, nall), 1) == lax.broadcasted_iota(jnp.int32, (nframe, nall), 0) + t * nframe
+    place = place.astype(jnp.float32)
+    keep8 = jnp.broadcast_to(keep_v[...], (8, nframe))
+    ids8 = jnp.broadcast_to(ids_v[...].astype(jnp.float32), (8, nframe))
+    pick = lax.broadcasted_iota(jnp.int32, (8, nframe), 0) == 0
+    both = jnp.where(pick, keep8, ids8)
+    small[0] = jnp.dot(both, place, precision=HI, preferred_element_type=jnp.float32)
+    pl.semaphore_wait(barrier, ntm + 1)
+
+    def rows(dev, core, q):
+        return pl.ds(dev * shard + core * (2 * part) + q * part, part)
+
+    def send(source, dest, index, device):
+        return pltpu.make_async_remote_copy(
+            src_ref=source, dst_ref=dest, send_sem=sw.at[index], recv_sem=rw.at[index],
+            device_id=device, device_id_type=MESH)
+
+    own = {}
+    for q in range(2):
+        source = w_time.at[:, pl.ds(c * (2 * part) + q * part, part)]
+        dest = w_full.at[:, rows(d, c, q)]
+        own[q] = send(source, dest, q, (xd, t))
+        own[2 + q] = send(source, dest, 2 + q, (yd, t))
+        own[q].start()
+        own[2 + q].start()
+    tail = pltpu.make_async_remote_copy(
+        src_ref=clips.at[pl.ds(nframe - halo, halo)], dst_ref=prior, send_sem=st, recv_sem=rt,
+        device_id=(d, lax.rem(t + 1, ntm)), device_id_type=MESH)
+
+    @pl.when(t < ntm - 1)
+    def _():
+        tail.start()
+
+    smalls = []
+    for k in range(1, ntm):
+        copy = pltpu.make_async_remote_copy(
+            src_ref=small.at[0], dst_ref=small.at[k], send_sem=sk.at[k - 1], recv_sem=rk.at[k - 1],
+            device_id=(d, lax.rem(t + k, ntm)), device_id_type=MESH)
+        copy.start()
+        smalls.append(copy)
+
+    @pl.when(t == 0)
+    def _():
+        zeros[...] = jnp.zeros_like(zeros)
+        for h in range(halo):
+            fill = pltpu.make_async_copy(zeros, prior.at[h], local_sem.at[1])
+            fill.start()
+            fill.wait()
+
+    for copy in smalls:
+        copy.wait_recv()
+    table = small[0]
+    for k in range(1, ntm):
+        table = table + small[k]
+
+    diag = 3 - d
+    got = {}
+    def forward(dev, q, index, device):
+        piece = w_full.at[:, rows(dev, c, q)]
+        copy = send(piece, piece, index, device)
+        copy.start()
+        got[index] = copy
+
+    own[0].wait_recv()
+    forward(xd, 0, 4, (yd, t))
+    forward(xd, 0, 6, (d, sister))
+    own[3].wait_recv()
+    forward(yd, 1, 5, (xd, t))
+    forward(yd, 1, 9, (d, sister))
+    own[1].wait_recv()
+    forward(xd, 1, 7, (d, sister))
+    own[2].wait_recv()
+    forward(yd, 0, 8, (d, sister))
+
+    maps_of(nframe, nlat, t * nframe, table[0:1], table[1:2].astype(jnp.int32),
+            lambda g: keep_s[g], lambda g: ids_s[g], rate[...], gain[...], w_lat[...], maps)
+
+    got[4].wait_recv()
+    forward(diag, 0, 10, (d, sister))
+    got[5].wait_recv()
+    forward(diag, 1, 11, (d, sister))
+    for index in range(6, 12):
+        got[index].wait_recv()
+    for index in range(4):
+        own[index].wait_send()
+    for index in range(4, 12):
+        got[index].wait_send()
+    for copy in smalls:
+        copy.wait_send()
+    own_copy.wait()
+
+    @pl.when(t < ntm - 1)
+    def _():
+        tail.wait_send()
+
+    @pl.when(t > 0)
+    def _():
+        tail.wait_recv()
+
+
+def gather_call(clips, w_time, gain, rate, keep, ids, w_lat):
+    nframe, npos, nchan = clips.shape
+    ntm = lax.axis_size("tm")
+    nall = nframe * ntm
+    nlat = nall // STRIDE
+    ncol = nlat * w_lat.shape[1]
+    any_spec = pl.BlockSpec(memory_space=pl.ANY)
+    smem = pl.BlockSpec(memory_space=pltpu.SMEM)
+    vmem = pl.BlockSpec(memory_space=pltpu.VMEM)
+    return pl.pallas_call(
+        functools.partial(gather_kernel, ntm, nlat),
+        out_shape=(
+            jax.ShapeDtypeStruct((KT, nchan, nchan), jnp.bfloat16),
+            jax.ShapeDtypeStruct((KT - 1, npos, nchan), jnp.bfloat16),
+            jax.ShapeDtypeStruct((nframe, nchan, ncol), jnp.bfloat16),
+        ),
+        in_specs=[any_spec, any_spec, smem, smem] + [vmem] * 5,
+        out_specs=(any_spec, any_spec, vmem),
+        scratch_shapes=[
+            pltpu.VMEM((ntm, 8, nall), jnp.float32),
+            pltpu.VMEM((npos, nchan), jnp.bfloat16),
+            pltpu.SemaphoreType.DMA((2,)),
+            pltpu.SemaphoreType.DMA((12,)),
+            pltpu.SemaphoreType.DMA((12,)),
+            pltpu.SemaphoreType.DMA,
+            pltpu.SemaphoreType.DMA,
+            pltpu.SemaphoreType.DMA((ntm - 1,)),
+            pltpu.SemaphoreType.DMA((ntm - 1,)),
+        ],
+        compiler_params=pltpu.CompilerParams(
+            collective_id=0, has_side_effects=True, vmem_limit_bytes=60 * 1024 * 1024),
+    )(clips, w_time, keep, ids, keep[None], ids[None], rate[None], gain[None], w_lat)
 
 
 def main_kernel(rows, clips, prior, w, maps, features, acc, xbuf, sems):
@@ -115,28 +266,80 @@
     )(clips, prior, w, maps)
 
 
+def reduce_kernel(nchip, per, acc, out, mine, theirs, sums, slots, s1, r1, s2, r2):
+    d, t = lax.axis_index("dp"), lax.axis_index("tm")
+    c = lax.rem(t, 2)
+    z = lax.div(t, 2)
+    sister = t + 1 - 2 * c
+    barrier = pltpu.get_barrier_semaphore()
+    pl.semaphore_signal(barrier, inc=1, device_id=(d, sister), device_id_type=MESH)
+    for k in range(1, nchip):
+        pl.semaphore_signal(barrier, inc=1, device_id=(d, lax.rem(z + k, nchip) * 2 + c), device_id_type=MESH)
+    turned = acc[...].T
+    for e in range(2 * nchip):
+        mine[e % 2, e // 2] = turned[e * per:(e + 1) * per]
+    pl.semaphore_wait(barrier, nchip)
+    swap = pltpu.make_async_remote_copy(
+        src_ref=mine.at[1 - c], dst_ref=theirs, send_sem=s1, recv_sem=r1,
+        device_id=(d, sister), device_id_type=MESH)
+    swap.start()
+    swap.wait_recv()
+    sums[...] = (mine[c] + theirs[...]).astype(jnp.bfloat16)
+
+    def copy(k):
+        ahead = lax.rem(z + k, nchip)
+        return pltpu.make_async_remote_copy(
+            src_ref=sums.at[ahead], dst_ref=slots.at[k - 1], send_sem=s2.at[k - 1], recv_sem=r2.at[k - 1],
+            device_id=(d, ahead * 2 + c), device_id_type=MESH)
+
+    for k in range(nchip - 1, 0, -1):
+        @pl.when(z + k < nchip)
+        def _():
+            copy(k).start()
+    out[...] = mine[c, z] + theirs[z]
+    for k in range(1, nchip):
+        @pl.when(z >= k)
+        def _():
+            copy(k).wait_recv()
+            out[...] += slots[k - 1].astype(jnp.float32)
+    for k in range(1, nchip):
+        @pl.when(z + k < nchip)
+        def _():
+            copy(k).wait_send()
+    swap.wait_send()
+
+
+def reduce_call(acc, per):
+    npos, ncol = acc.shape
+    nchip = lax.axis_size("tm") // 2
+    vmem = pl.BlockSpec(memory_space=pltpu.VMEM)
+    return pl.pallas_call(
+        functools.partial(reduce_kernel, nchip, per),
+        out_shape=jax.ShapeDtypeStruct((per, npos), jnp.float32),
+        in_specs=[vmem],
+        out_specs=vmem,
+        scratch_shapes=[
+            pltpu.VMEM((2, nchip, per, npos), jnp.float32),
+            pltpu.VMEM((nchip, per, npos), jnp.float32),
+            pltpu.VMEM((nchip, per, npos), jnp.bfloat16),
+            pltpu.VMEM((nchip - 1, per, npos), jnp.bfloat16),
+            pltpu.SemaphoreType.DMA,
+            pltpu.SemaphoreType.DMA,
+            pltpu.SemaphoreType.DMA((nchip - 1,)),
+            pltpu.SemaphoreType.DMA((nchip - 1,)),
+        ],
+        compiler_params=pltpu.CompilerParams(
+            collective_id=1, has_side_effects=True, vmem_limit_bytes=48 * 1024 * 1024),
+    )(acc)
+
+
 def per_device(clips, w_time, gain, rate, keep, latent_ids, w_lat):
     nclip, nframe, npos, nchan = clips.shape
-    ntm = lax.axis_size("tm")
-    nlat = nframe * ntm // STRIDE
+    nown = nframe // STRIDE
     latc = w_lat.shape[1]
-    halo = KT - 1
-    tail = clips[:, nframe - halo:]
-    prior = lax.ppermute(tail, "tm", [(s, s + 1) for s in range(ntm - 1)])[0]
-    w = lax.all_gather(w_time, "dp", axis=1, tiled=True).reshape(KT * nchan, nchan)
-    keep_all = lax.all_gather(keep, "tm", tiled=True)
-    ids_all = lax.all_gather(latent_ids, "tm", tiled=True)
-    wl = jnp.tile(w_lat.astype(jnp.float32), (1, nlat))
-    maps = pl.pallas_call(
-        functools.partial(maps_kernel, nlat),
-        out_shape=jax.ShapeDtypeStruct((nframe, nchan, nlat * latc), jnp.bfloat16),
-        in_specs=[pl.BlockSpec(memory_space=pltpu.SMEM)] * 2 + [pl.BlockSpec(memory_space=pltpu.VMEM)] * 5,
-        out_specs=pl.BlockSpec(memory_space=pltpu.VMEM),
-        compiler_params=pltpu.CompilerParams(vmem_limit_bytes=60 * 1024 * 1024),
-    )(keep, latent_ids, keep_all[None], ids_all[None], rate[:, None], gain[:, None], wl)
-    features, acc = main_call(clips[0], prior, w, maps)
-    share = acc.T.reshape(nlat, latc, npos)
-    latents = lax.psum_scatter(share, "tm", scatter_dimension=0, tiled=True)
+    w, prior, maps = gather_call(clips[0], w_time, gain, rate, keep, latent_ids, w_lat)
+    features, acc = main_call(clips[0], prior, w.reshape(KT * nchan, nchan), maps)
+    latents = reduce_call(acc, nown * latc).reshape(nown, latc, npos)
     return (features[None], latents[None])
 
 

time: 116 us -> 65.8 us (0.57)
  the two profiles are of different devices: /device:TPU:0 before, /device:TPU:17 now
where the time goes in v2:
time: 65.8 us; the launch traced here: 64.6 us
  Pallas kernels  59.2 us (90%)
  local copies, waits for them, and re-layouts  4.73 us (7%)
  between operations  0.66 us (1%)
    pallas_call x1, Pallas kernels, gather_call(): pl.pallas_call(functools.partial(gather_kernel, ntm, nlat), out_shape=(ja...  27 us
    pallas_call x1, Pallas kernels, main_call(): pl.pallas_call(functools.partial(main_kernel, rows), grid=(nframe,), out_...  24.4 us
    pallas_call x1, Pallas kernels, reduce_call(): pl.pallas_call(functools.partial(reduce_kernel, nchip, per), out_shape=ja...  7.81 us
    unnamed x6, local copies, waits for them, and re-layouts  4.73 us

profile of v2, /device:TPU:17, one launch (start us, length us, event | category | flops | bytes accessed | tf_op | source)
XLA Modules:
  0.0 64.6 jit_solution(8019468441574132542)
XLA Ops:
  0.6 1.5 %copy.9.w_lat = bf16[512,16]{1,0:T(8,128)(2,1)} copy(bf16[512,16]{0,1:T(8,128)(2,1)} %param.13) | data formatting | bytes 32768 | tf_op args[6]
  2.1 27.0 %shard_map.86 = (bf16[3,512,512]{2,1,0:T(8,128)(2,1)}, bf16[2,512,512]{2,1,0:T(8,128)(2,1)}, bf16[16,512,256]{2,1,0:T(8,128)(2,1)}) custom-call(bf16[16,512,512]{2,1,0:T(8,128)(2,1)} %bitcast.10, bf16[3,128,512]{2,1,0:T(8,128)(2,1)} %w_time.1, f32[16]{0:T(128)} %keep_s.1, s32[16]{0:T(128)} %ids_s.1, f32[1,16]{1,0:T(1,128)} %bitcast.14, s32[1,16]{1,0:T(1,128)} %bitcast.15, ...), custom_call_target="tpu_custom_call" | custom-call | tf_op jit(solution)/shard_map/pallas_call | solution.py:183
  29.1 0.0 copy-start
  29.1 1.4 %copy-done = bf16[3,512,512]{2,1,0:T(8,128)(2,1)S(1)} copy-done((bf16[3,512,512]{2,1,0:T(8,128)(2,1)S(1)}, bf16[3,512,512]{2,1,0:T(8,128)(2,1)}, u32[]{:S(2)}) %copy-start) | copy-done | bytes 1572888
  30.5 0.0 copy-start.1
  30.5 1.2 %copy-done.1 = bf16[2,512,512]{2,1,0:T(8,128)(2,1)S(1)} copy-done((bf16[2,512,512]{2,1,0:T(8,128)(2,1)S(1)}, bf16[2,512,512]{2,1,0:T(8,128)(2,1)}, u32[]{:S(2)}) %copy-start.1) | copy-done | bytes 1048600
  31.8 24.4 %shard_map.87 = (bf16[16,512,512]{2,1,0:T(8,128)(2,1)}, f32[512,256]{1,0:T(8,128)S(1)}) custom-call(bf16[16,512,512]{2,1,0:T(8,128)(2,1)} %bitcast.11, bf16[2,512,512]{2,1,0:T(8,128)(2,1)S(1)} %copy-done.1, bf16[1536,512]{1,0:T(8,128)(2,1)S(1)} %bitcast.8, bf16[16,512,256]{2,1,0:T(8,128)(2,1)} %get-tuple-element.9.maps), custom_call_target="tpu_custom_call" | custom-call | tf_op jit(solution)/shard_map/pallas_call | solution.py:244
  56.1 7.8 %shard_map.88 = f32[32,512]{1,0:T(8,128)S(1)} custom-call(f32[512,256]{1,0:T(8,128)S(1)} %get-tuple-element.11.acc), custom_call_target="tpu_custom_call" | custom-call | tf_op jit(solution)/shard_map/pallas_call | solution.py:316
  64.0 0.6 copy.11
Async XLA Ops:
  29.1 1.4 %copy-start = (bf16[3,512,512]{2,1,0:T(8,128)(2,1)S(1)}, bf16[3,512,512]{2,1,0:T(8,128)(2,1)}, u32[]{:S(2)}) copy-start(bf16[3,512,512]{2,1,0:T(8,128)(2,1)} %get-tuple-element.8) | copy-start | bytes 4718596
  30.5 1.2 %copy-start.1 = (bf16[2,512,512]{2,1,0:T(8,128)(2,1)S(1)}, bf16[2,512,512]{2,1,0:T(8,128)(2,1)}, u32[]{:S(2)}) copy-start(bf16[2,512,512]{2,1,0:T(8,128)(2,1)} %get-tuple-element.7.prior) | copy-start | bytes 3145732

commit v3 on v2

--- a/solution.py
+++ b/solution.py
@@ -15,14 +15,14 @@
 MESH = pl.DeviceIdType.MESH
 
 
-def maps_of(nframe, nlat, base, keep_row, ids_row, keep_own, ids_own, rate_row, gain_row, w_lat, out_ref):
+def maps_of(nframe, nlat, base, keep_row, ids_row, keep_own, ids_own, rate_row, gain_row, w_lat, maps_ref):
     nall = keep_row.shape[1]
-    nchan, latc = w_lat.shape
+    latc, nchan = w_lat.shape
     ncol = nlat * latc
     rate_col = jnp.broadcast_to(rate_row, (128, nchan)).T[:, :1]
     gain_col = jnp.broadcast_to(gain_row, (128, nchan)).T[:, :1]
     spread = lax.broadcasted_iota(jnp.int32, (latc, ncol), 1) % latc == lax.broadcasted_iota(jnp.int32, (latc, ncol), 0)
-    wl = jnp.dot(w_lat, spread.astype(jnp.bfloat16), preferred_element_type=jnp.float32)
+    wl = lax.dot_general(w_lat, spread.astype(jnp.bfloat16), (((0,), (0,)), ((), ())), preferred_element_type=jnp.float32)
     end = base + nframe - 1
     frame = lax.broadcasted_iota(jnp.int32, (8, nall), 1)
     later = frame > end
@@ -42,13 +42,18 @@
     weight = wl * (inject * gain_col) / counts
     decay = jnp.exp(-rate_col)
     column = lax.broadcasted_iota(jnp.int32, (1, ncol), 1) // latc
-    here = (column == ids_own(nframe - 1)).astype(jnp.float32)
-    total = here + entry
-    out_ref[nframe - 1] = (weight * total).astype(jnp.bfloat16)
-    for g in range(nframe - 2, -1, -1):
-        here = (column == ids_own(g)).astype(jnp.float32)
-        total = here + (decay * keep_own(g + 1)) * total
-        out_ref[g] = (weight * total).astype(jnp.bfloat16)
+    here = [(column == ids_own(g)).astype(jnp.float32) for g in range(nframe)]
+    yield
+    chunk = nchan // 4
+    for at in range(0, nchan, chunk):
+        span = slice(at, at + chunk)
+        scale, fade = weight[span], decay[span]
+        total = here[nframe - 1] + entry[span]
+        maps_ref[nframe - 1, span] = (scale * total).astype(jnp.bfloat16)
+        for g in range(nframe - 2, -1, -1):
+            total = here[g] + (fade * keep_own(g + 1)) * total
+            maps_ref[g, span] = (scale * total).astype(jnp.bfloat16)
+        yield
 
 
 def gather_kernel(ntm, nlat, clips, w_time, keep_s, ids_s, keep_v, ids_v, rate, gain, w_lat,
@@ -88,22 +93,6 @@
             src_ref=source, dst_ref=dest, send_sem=sw.at[index], recv_sem=rw.at[index],
             device_id=device, device_id_type=MESH)
 
-    own = {}
-    for q in range(2):
-        source = w_time.at[:, pl.ds(c * (2 * part) + q * part, part)]
-        dest = w_full.at[:, rows(d, c, q)]
-        own[q] = send(source, dest, q, (xd, t))
-        own[2 + q] = send(source, dest, 2 + q, (yd, t))
-        own[q].start()
-        own[2 + q].start()
-    tail = pltpu.make_async_remote_copy(
-        src_ref=clips.at[pl.ds(nframe - halo, halo)], dst_ref=prior, send_sem=st, recv_sem=rt,
-        device_id=(d, lax.rem(t + 1, ntm)), device_id_type=MESH)
-
-    @pl.when(t < ntm - 1)
-    def _():
-        tail.start()
-
     smalls = []
     for k in range(1, ntm):
         copy = pltpu.make_async_remote_copy(
@@ -112,6 +101,22 @@
         copy.start()
         smalls.append(copy)
 
+    own = {}
+    for q in range(2):
+        source = w_time.at[:, pl.ds(c * (2 * part) + q * part, part)]
+        dest = w_full.at[:, rows(d, c, q)]
+        own[q] = send(source, dest, q, (xd, t))
+        own[2 + q] = send(source, dest, 2 + q, (yd, t))
+    for index in (0, 3, 1, 2):
+        own[index].start()
+    tail = pltpu.make_async_remote_copy(
+        src_ref=clips.at[pl.ds(nframe - halo, halo)], dst_ref=prior, send_sem=st, recv_sem=rt,
+        device_id=(d, lax.rem(t + 1, ntm)), device_id_type=MESH)
+
+    @pl.when(t < ntm - 1)
+    def _():
+        tail.start()
+
     @pl.when(t == 0)
     def _():
         zeros[...] = jnp.zeros_like(zeros)
@@ -134,24 +139,27 @@
         copy.start()
         got[index] = copy
 
+    making = maps_of(nframe, nlat, t * nframe, table[0:1], table[1:2].astype(jnp.int32),
+                     lambda g: keep_s[g], lambda g: ids_s[g], rate[...], gain[...], w_lat[...], maps)
+    next(making)
     own[0].wait_recv()
     forward(xd, 0, 4, (yd, t))
     forward(xd, 0, 6, (d, sister))
     own[3].wait_recv()
     forward(yd, 1, 5, (xd, t))
     forward(yd, 1, 9, (d, sister))
+    next(making)
     own[1].wait_recv()
     forward(xd, 1, 7, (d, sister))
     own[2].wait_recv()
     forward(yd, 0, 8, (d, sister))
-
-    maps_of(nframe, nlat, t * nframe, table[0:1], table[1:2].astype(jnp.int32),
-            lambda g: keep_s[g], lambda g: ids_s[g], rate[...], gain[...], w_lat[...], maps)
-
+    next(making)
+    next(making)
     got[4].wait_recv()
     forward(diag, 0, 10, (d, sister))
     got[5].wait_recv()
     forward(diag, 1, 11, (d, sister))
+    next(making)
     for index in range(6, 12):
         got[index].wait_recv()
     for index in range(4):
@@ -202,13 +210,13 @@
         ],
         compiler_params=pltpu.CompilerParams(
             collective_id=0, has_side_effects=True, vmem_limit_bytes=60 * 1024 * 1024),
-    )(clips, w_time, keep, ids, keep[None], ids[None], rate[None], gain[None], w_lat)
-
-
-def main_kernel(rows, clips, prior, w, maps, features, acc, xbuf, sems):
+    )(clips, w_time, keep, ids, keep[None], ids[None], rate[None], gain[None], w_lat.T)
+
+
+def main_kernel(rows, per, clips, prior, w, maps, features, acc, xbuf, sems):
     step = pl.program_id(0)
     nframe = clips.shape[0]
-    npos = clips.shape[1]
+    npos, nchan = clips.shape[1:]
     halo = KT - 1
 
     def load(slot):
@@ -223,27 +231,45 @@
             load(slot).wait()
         acc[...] = jnp.zeros_like(acc)
 
-    pltpu.make_async_copy(clips.at[step], xbuf.at[step + halo], sems.at[step + halo]).wait()
-    for at in range(0, npos, rows):
-        span = slice(at, at + rows)
-        own = xbuf[step + halo, span]
-        lhs = jnp.concatenate([own] + [xbuf[step + halo - k, span] for k in range(1, KT)], axis=1)
-        half = 0.5 * jnp.dot(lhs, w[...], preferred_element_type=jnp.float32)
+    first = step * per
+    for k in range(per):
+        at = first + k
+        pltpu.make_async_copy(clips.at[at], xbuf.at[at + halo], sems.at[at + halo]).wait()
+
+    def conv(at):
+        span = pl.ds(at, rows)
+        taps = [xbuf[pl.ds(first + halo - k, per), span].reshape(per * rows, nchan) for k in range(KT)]
+        return taps[0], jnp.dot(jnp.concatenate(taps, axis=1), w[...], preferred_element_type=jnp.float32)
+
+    def post(at, own, total):
+        span = pl.ds(at, rows)
+        half = 0.5 * total
         value = own.astype(jnp.float32) + (half * jnp.tanh(half) + half)
         rounded = value.astype(jnp.bfloat16)
-        features[0, span] = rounded
-        kept = rounded.astype(jnp.float32)
-        scale = lax.rsqrt(jnp.mean(kept * kept, axis=-1, keepdims=True) + 1e-06)
-        acc[span] += scale * jnp.dot(rounded, maps[0], preferred_element_type=jnp.float32)
-
-
-def main_call(clips, prior, w, maps, rows=512):
+        features[:, span] = rounded.reshape(per, rows, nchan)
+        scale = lax.rsqrt(jnp.mean(value * value, axis=-1, keepdims=True) + 1e-06)
+        out = acc[span]
+        for k in range(per):
+            part = slice(k * rows, (k + 1) * rows)
+            out = out + scale[part] * jnp.dot(rounded[part], maps[k], preferred_element_type=jnp.float32)
+        acc[span] = out
+
+    held = None
+    for at in range(0, npos, rows):
+        now = conv(at)
+        if held is not None:
+            post(*held)
+        held = (at, *now)
+    post(*held)
+
+
+def main_call(clips, prior, w, maps, rows=512, per=2):
     nframe, npos, nchan = clips.shape
     ncol = maps.shape[-1]
     halo = KT - 1
     return pl.pallas_call(
-        functools.partial(main_kernel, rows),
-        grid=(nframe,),
+        functools.partial(main_kernel, rows, per),
+        grid=(nframe // per,),
         out_shape=(
             jax.ShapeDtypeStruct((nframe, npos, nchan), jnp.bfloat16),
             jax.ShapeDtypeStruct((npos, ncol), jnp.float32),
@@ -252,17 +278,17 @@
             pl.BlockSpec(memory_space=pl.ANY),
             pl.BlockSpec(memory_space=pl.ANY),
             pl.BlockSpec(w.shape, lambda i: (0, 0)),
-            pl.BlockSpec((1, nchan, ncol), lambda i: (i, 0, 0)),
+            pl.BlockSpec((per, nchan, ncol), lambda i: (i, 0, 0)),
         ],
         out_specs=(
-            pl.BlockSpec((1, npos, nchan), lambda i: (i, 0, 0)),
+            pl.BlockSpec((per, npos, nchan), lambda i: (i, 0, 0)),
             pl.BlockSpec((npos, ncol), lambda i: (0, 0)),
         ),
         scratch_shapes=[
             pltpu.VMEM((nframe + halo, npos, nchan), jnp.bfloat16),
             pltpu.SemaphoreType.DMA((nframe + halo,)),
         ],
-        compiler_params=pltpu.CompilerParams(vmem_limit_bytes=48 * 1024 * 1024),
+        compiler_params=pltpu.CompilerParams(vmem_limit_bytes=56 * 1024 * 1024),
     )(clips, prior, w, maps)
 
 

time: 65.8 us -> 53.6 us (0.81); the launches traced: 64.6 us -> 53.3 us
  Pallas kernels: 59.2 us -> 51 us
  local copies, waits for them, and re-layouts: 4.73 us -> 1.67 us
    pallas_call x1, Pallas kernels: 27 us -> 17.6 us  [gather_call(): pl.pallas_call(functools.partial(gather_kernel, ntm, nlat), out_shape=(ja...]
    unnamed x6 -> x3, local copies, waits for them, and re-layouts: 4.73 us -> 1.67 us
    pallas_call x1, Pallas kernels: 7.81 us -> 9.09 us  [reduce_call(): pl.pallas_call(functools.partial(reduce_kernel, nchip, per), out_shape=ja...]
where the time goes in v3:
time: 53.6 us; the launch traced here: 53.3 us
  Pallas kernels  51 us (95%)
  local copies, waits for them, and re-layouts  1.67 us (3%)
  between operations  0.66 us (1%)
    pallas_call x1, Pallas kernels, main_call(): pl.pallas_call(functools.partial(main_kernel, rows, per), grid=(nframe //...  24.3 us
    pallas_call x1, Pallas kernels, gather_call(): pl.pallas_call(functools.partial(gather_kernel, ntm, nlat), out_shape=(ja...  17.6 us
    pallas_call x1, Pallas kernels, reduce_call(): pl.pallas_call(functools.partial(reduce_kernel, nchip, per), out_shape=ja...  9.09 us
    unnamed x3, local copies, waits for them, and re-layouts  1.67 us

profile of v3, /device:TPU:17, one launch (start us, length us, event | category | flops | bytes accessed | tf_op | source)
XLA Modules:
  0.0 53.3 jit_solution(5978117807268720046)
XLA Ops:
  0.6 17.6 %shard_map.86 = (bf16[3,512,512]{2,1,0:T(8,128)(2,1)}, bf16[2,512,512]{2,1,0:T(8,128)(2,1)}, bf16[16,512,256]{2,1,0:T(8,128)(2,1)}) custom-call(bf16[16,512,512]{2,1,0:T(8,128)(2,1)} %bitcast.10, bf16[3,128,512]{2,1,0:T(8,128)(2,1)} %w_time.1, f32[16]{0:T(128)} %keep_s.1, s32[16]{0:T(128)} %ids_s.1, f32[1,16]{1,0:T(1,128)} %bitcast.16, s32[1,16]{1,0:T(1,128)} %bitcast.17, ...), custom_call_target="tpu_custom_call" | custom-call | tf_op jit(solution)/shard_map/pallas_call | solution.py:191
  18.3 24.3 %shard_map.87 = (bf16[16,512,512]{2,1,0:T(8,128)(2,1)}, f32[512,256]{1,0:T(8,128)}) custom-call(bf16[16,512,512]{2,1,0:T(8,128)(2,1)} %bitcast.11, bf16[2,512,512]{2,1,0:T(8,128)(2,1)} %get-tuple-element.7.prior, bf16[1536,512]{1,0:T(8,128)(2,1)} %bitcast.12, bf16[16,512,256]{2,1,0:T(8,128)(2,1)} %get-tuple-element.9.maps), custom_call_target="tpu_custom_call" | custom-call | tf_op jit(solution)/shard_map/pallas_call | solution.py:270
  42.6 0.0 copy-start
  42.6 1.0 %copy-done = f32[512,256]{1,0:T(8,128)S(1)} copy-done((f32[512,256]{1,0:T(8,128)S(1)}, f32[512,256]{1,0:T(8,128)}, u32[]{:S(2)}) %copy-start) | copy-done | bytes 524312
  43.6 9.1 %shard_map.88 = f32[32,512]{1,0:T(8,128)S(1)} custom-call(f32[512,256]{1,0:T(8,128)S(1)} %copy-done), custom_call_target="tpu_custom_call" | custom-call | tf_op jit(solution)/shard_map/pallas_call | solution.py:342
  52.7 0.6 %copy.10 = f32[1,2,16,512]{3,2,1,0:T(8,128)} copy(f32[1,2,16,512]{3,2,1,0:T(8,128)S(1)} %bitcast.9) | data formatting | bytes 131072
Async XLA Ops:
  42.6 1.0 %copy-start = (f32[512,256]{1,0:T(8,128)S(1)}, f32[512,256]{1,0:T(8,128)}, u32[]{:S(2)}) copy-start(f32[512,256]{1,0:T(8,128)} %get-tuple-element.11.acc) | copy-start | bytes 1572868

commit v4 on v3

--- a/solution.py
+++ b/solution.py
@@ -57,7 +57,7 @@
 
 
 def gather_kernel(ntm, nlat, clips, w_time, keep_s, ids_s, keep_v, ids_v, rate, gain, w_lat,
-                  w_full, prior, maps, small, zeros, local_sem, sw, rw, st, rt, sk, rk):
+                  w_full, prior, maps_out, maps, small, zeros, local_sem, map_sem, sw, rw, st, rt, sk, rk):
     halo = KT - 1
     nframe = clips.shape[0]
     shard = w_time.shape[1]
@@ -121,15 +121,7 @@
     def _():
         zeros[...] = jnp.zeros_like(zeros)
         for h in range(halo):
-            fill = pltpu.make_async_copy(zeros, prior.at[h], local_sem.at[1])
-            fill.start()
-            fill.wait()
-
-    for copy in smalls:
-        copy.wait_recv()
-    table = small[0]
-    for k in range(1, ntm):
-        table = table + small[k]
+            pltpu.make_async_copy(zeros, prior.at[h], local_sem.at[1 + h]).start()
 
     diag = 3 - d
     got = {}
@@ -139,27 +131,38 @@
         copy.start()
         got[index] = copy
 
-    making = maps_of(nframe, nlat, t * nframe, table[0:1], table[1:2].astype(jnp.int32),
-                     lambda g: keep_s[g], lambda g: ids_s[g], rate[...], gain[...], w_lat[...], maps)
-    next(making)
     own[0].wait_recv()
     forward(xd, 0, 4, (yd, t))
     forward(xd, 0, 6, (d, sister))
     own[3].wait_recv()
     forward(yd, 1, 5, (xd, t))
     forward(yd, 1, 9, (d, sister))
-    next(making)
     own[1].wait_recv()
     forward(xd, 1, 7, (d, sister))
     own[2].wait_recv()
     forward(yd, 0, 8, (d, sister))
-    next(making)
+
+    for copy in smalls:
+        copy.wait_recv()
+    table = small[0]
+    for k in range(1, ntm):
+        table = table + small[k]
+
+    making = maps_of(nframe, nlat, t * nframe, table[0:1], table[1:2].astype(jnp.int32),
+                     lambda g: keep_s[g], lambda g: ids_s[g], rate[...], gain[...], w_lat[...], maps)
     next(making)
     got[4].wait_recv()
     forward(diag, 0, 10, (d, sister))
     got[5].wait_recv()
     forward(diag, 1, 11, (d, sister))
-    next(making)
+    chunk = maps.shape[1] // 4
+    leaving = []
+    for k in range(4):
+        next(making)
+        span = pl.ds(k * chunk, chunk)
+        copy = pltpu.make_async_copy(maps.at[:, span], maps_out.at[:, span], map_sem.at[k])
+        copy.start()
+        leaving.append(copy)
     for index in range(6, 12):
         got[index].wait_recv()
     for index in range(4):
@@ -169,6 +172,13 @@
     for copy in smalls:
         copy.wait_send()
     own_copy.wait()
+    for copy in leaving:
+        copy.wait()
+
+    @pl.when(t == 0)
+    def _():
+        for h in range(halo):
+            pltpu.make_async_copy(zeros, prior.at[h], local_sem.at[1 + h]).wait()
 
     @pl.when(t < ntm - 1)
     def _():
@@ -196,11 +206,13 @@
             jax.ShapeDtypeStruct((nframe, nchan, ncol), jnp.bfloat16),
         ),
         in_specs=[any_spec, any_spec, smem, smem] + [vmem] * 5,
-        out_specs=(any_spec, any_spec, vmem),
+        out_specs=(any_spec, any_spec, any_spec),
         scratch_shapes=[
+            pltpu.VMEM((nframe, nchan, ncol), jnp.bfloat16),
             pltpu.VMEM((ntm, 8, nall), jnp.float32),
             pltpu.VMEM((npos, nchan), jnp.bfloat16),
-            pltpu.SemaphoreType.DMA((2,)),
+            pltpu.SemaphoreType.DMA((KT,)),
+            pltpu.SemaphoreType.DMA((4,)),
             pltpu.SemaphoreType.DMA((12,)),
             pltpu.SemaphoreType.DMA((12,)),
             pltpu.SemaphoreType.DMA,

time: 53.6 us -> 51.7 us (0.965)
  Pallas kernels: 51 us -> 49.1 us
    pallas_call x1, Pallas kernels: 17.6 us -> 15.7 us  [gather_call(): pl.pallas_call(functools.partial(gather_kernel, ntm, nlat), out_shape=(ja...]
where the time goes in v4:
time: 51.7 us; the launch traced here: 51.4 us
  Pallas kernels  49.1 us (95%)
  local copies, waits for them, and re-layouts  1.67 us (3%)
  between operations  0.66 us (1%)
    pallas_call x1, Pallas kernels, main_call(): pl.pallas_call(functools.partial(main_kernel, rows, per), grid=(nframe //...  24.3 us
    pallas_call x1, Pallas kernels, gather_call(): pl.pallas_call(functools.partial(gather_kernel, ntm, nlat), out_shape=(ja...  15.7 us
    pallas_call x1, Pallas kernels, reduce_call(): pl.pallas_call(functools.partial(reduce_kernel, nchip, per), out_shape=ja...  9.1 us
    unnamed x3, local copies, waits for them, and re-layouts  1.67 us

profile of v4, /device:TPU:17, one launch (start us, length us, event | category | flops | bytes accessed | tf_op | source)
XLA Modules:
  0.0 51.4 jit_solution(10312172992068142185)
XLA Ops:
  0.6 15.7 %shard_map.86 = (bf16[3,512,512]{2,1,0:T(8,128)(2,1)}, bf16[2,512,512]{2,1,0:T(8,128)(2,1)}, bf16[16,512,256]{2,1,0:T(8,128)(2,1)}) custom-call(bf16[16,512,512]{2,1,0:T(8,128)(2,1)} %bitcast.10, bf16[3,128,512]{2,1,0:T(8,128)(2,1)} %w_time.1, f32[16]{0:T(128)} %keep_s.1, s32[16]{0:T(128)} %ids_s.1, f32[1,16]{1,0:T(1,128)} %bitcast.16, s32[1,16]{1,0:T(1,128)} %bitcast.17, ...), custom_call_target="tpu_custom_call" | custom-call | tf_op jit(solution)/shard_map/pallas_call | solution.py:201
  16.4 24.3 %shard_map.87 = (bf16[16,512,512]{2,1,0:T(8,128)(2,1)}, f32[512,256]{1,0:T(8,128)}) custom-call(bf16[16,512,512]{2,1,0:T(8,128)(2,1)} %bitcast.11, bf16[2,512,512]{2,1,0:T(8,128)(2,1)} %get-tuple-element.7.prior, bf16[1536,512]{1,0:T(8,128)(2,1)} %bitcast.12, bf16[16,512,256]{2,1,0:T(8,128)(2,1)} %get-tuple-element.9.maps), custom_call_target="tpu_custom_call" | custom-call | tf_op jit(solution)/shard_map/pallas_call | solution.py:282
  40.7 0.0 copy-start
  40.7 1.0 %copy-done = f32[512,256]{1,0:T(8,128)S(1)} copy-done((f32[512,256]{1,0:T(8,128)S(1)}, f32[512,256]{1,0:T(8,128)}, u32[]{:S(2)}) %copy-start) | copy-done | bytes 524312
  41.7 9.1 %shard_map.88 = f32[32,512]{1,0:T(8,128)S(1)} custom-call(f32[512,256]{1,0:T(8,128)S(1)} %copy-done), custom_call_target="tpu_custom_call" | custom-call | tf_op jit(solution)/shard_map/pallas_call | solution.py:354
  50.8 0.6 %copy.10 = f32[1,2,16,512]{3,2,1,0:T(8,128)} copy(f32[1,2,16,512]{3,2,1,0:T(8,128)S(1)} %bitcast.9) | data formatting | bytes 131072
Async XLA Ops:
  40.7 1.0 %copy-start = (f32[512,256]{1,0:T(8,128)S(1)}, f32[512,256]{1,0:T(8,128)}, u32[]{:S(2)}) copy-start(f32[512,256]{1,0:T(8,128)} %get-tuple-element.11.acc) | copy-start | bytes 1572868
